TPU v7x, 32 devices: a whole 2x2x4 slice. The times are simulated.
32 devices in a mesh: cases: 2 (over y), blocks: 4 (over z), split: 2 (over x), inner: 2 (over core).
Axes of the slice: x: 2, y: 2, z: 4, core: 2. Of those that a mesh axis runs over, the one named last changes fastest.
Arguments:
- state: float32 [5, 64, 16, 256], P(None, ('cases', 'blocks', 'split', 'inner')), parts along dimension 1, may hold values from -2 to 5, as said below
- metrics: float32 [9, 32, 16, 256], P(None, ('blocks', 'split', 'inner')), may hold values from -1 to 1
- inv_volume: float32 [32, 16, 256], P(('blocks', 'split', 'inner')), may hold values from 0.5 to 1.5
- iblank: int32 [32, 16, 256], P(('blocks', 'split', 'inner')), may hold values 0 or 1
- donor_cells: int32 [16, 8, 256], P(('blocks', 'split', 'inner')), may hold values from 0 to 8191, as said below
- donor_fracs: float32 [16, 3, 256], P(('blocks', 'split', 'inner')), may hold values from 0 to 1
- receiver_cells: int32 [16, 256], P(('blocks', 'split', 'inner')), may hold values from 0 to 8192, as said below
Outputs:
- new_state: float32 [5, 64, 16, 256], P(None, ('cases', 'blocks', 'split', 'inner')), parts along dimension 1
There are 2 independent parts, one for each index of `cases`. A program takes and returns all parts, laid end to end along the dimension named above; an argument that names none is the same for every part. Nothing has to cross between parts.
Inputs may be any that keep to these rules, and one draw needn't show every extreme that they name: `state`: density and pressure are positive; the gas has a ratio of specific heats of 1.4. `donor_cells`: each slot's eight entries are the corners of one hexahedron of the owner's cells: entry c lies at offsets (c // 4, (c // 2) % 2, c % 2) along the three dimensions from entry 0. Slot r * 16 + q serves receiving device r. `receiver_cells`: on each receiving device the entries below 8192 are distinct cells; an entry equal to 8192 is an unused slot. Among the 16 slots from one owner, the used ones come first.
All inputs are finite; a program needn't handle non-finite values. No bound on the sum of `iblank` on one device may be relied on, other than what follows from the above.
Results may differ from a plain program's by a relative error of at most 0.00002.
Values sent between devices are 32-bit elements; how exact they have to be, the bound alone decides.
A program may use at most 64 MiB of HBM per device.

v0:
```python
import jax
import jax.numpy as jnp
from jax import lax
from jax.sharding import PartitionSpec as P

HEAT_RATIO = 1.4
TIME_STEP = 0.08


def extended_2(cells, sides, width):
    for axis, dim in sides:
        count = lax.axis_size(axis)
        ends = count - 1
        head = lax.slice_in_dim(cells, 0, width, axis=dim)
        tail = lax.slice_in_dim(cells, cells.shape[dim] - width, cells.shape[dim], axis=dim)
        cells = jnp.concatenate(
            [
                lax.ppermute(tail, axis, [(i, (i + 1) % count) for i in range(ends)]),
                cells,
                lax.ppermute(head, axis, [((i + 1) % count, i) for i in range(ends)]),
            ],
            axis=dim,
        )
    return cells


def edge_padded(field, axis):
    length = field.shape[axis]
    lower = lax.slice_in_dim(field, 0, 1, axis=axis)
    upper = lax.slice_in_dim(field, length - 1, length, axis=axis)
    return jnp.concatenate([lower, field, upper], axis=axis)


def fluxes(state, normal):
    density = state[0]
    momentum = state[1:4]
    energy = state[4]
    velocity = momentum / density
    pressure = (HEAT_RATIO - 1.0) * (energy - 0.5 * jnp.sum(momentum * velocity, axis=0))
    normal_speed = jnp.sum(velocity * normal, axis=0)
    face_flux = jnp.stack(
        [
            density * normal_speed,
            momentum[0] * normal_speed + pressure * normal[0],
            momentum[1] * normal_speed + pressure * normal[1],
            momentum[2] * normal_speed + pressure * normal[2],
            (energy + pressure) * normal_speed,
        ]
    )
    radius = jnp.abs(normal_speed) + jnp.sqrt(
        HEAT_RATIO * pressure / density * jnp.sum(normal * normal, axis=0)
    )
    return (face_flux, radius)


def face_difference(state_ext, normal_ext, axis):
    face_count = state_ext.shape[axis] - 1
    left_state = lax.slice_in_dim(state_ext, 0, face_count, axis=axis)
    right_state = lax.slice_in_dim(state_ext, 1, face_count + 1, axis=axis)
    normal = 0.5 * (
        lax.slice_in_dim(normal_ext, 0, face_count, axis=axis)
        + lax.slice_in_dim(normal_ext, 1, face_count + 1, axis=axis)
    )
    left_flux, left_radius = fluxes(left_state, normal)
    right_flux, right_radius = fluxes(right_state, normal)
    face_flux = 0.5 * (left_flux + right_flux) - 0.5 * jnp.maximum(left_radius, right_radius)[
        None
    ] * (right_state - left_state)
    return lax.slice_in_dim(face_flux, 1, face_count, axis=axis) - lax.slice_in_dim(
        face_flux, 0, face_count - 1, axis=axis
    )


def residual_rate(state, state_ext, normal_ext, metrics, inv_volume):
    summed = face_difference(state_ext, normal_ext, 1)
    summed = summed + face_difference(edge_padded(state, 2), edge_padded(metrics[3:6], 2), 2)
    summed = summed + face_difference(edge_padded(state, 3), edge_padded(metrics[6:9], 3), 3)
    return -inv_volume[None] * summed


def corner_weights(fractions):
    stacked = []
    for corner in range(8):
        factor = jnp.ones_like(fractions[0])
        for direction, offset_bit in ((0, corner // 4), (1, corner // 2 % 2), (2, corner % 2)):
            factor = factor * (fractions[direction] if offset_bit else 1.0 - fractions[direction])
        stacked.append(factor)
    return jnp.stack(stacked)


def extend_across(extended, field):
    position = lax.axis_index(("split", "inner"))
    last_index = lax.axis_size(("split", "inner")) - 1
    lower_ghost = jnp.where(position == 0, field[:, :1], extended[:, :1])
    upper_ghost = jnp.where(position == last_index, field[:, -1:], extended[:, -1:])
    return jnp.concatenate([lower_ghost, field, upper_ghost], axis=1)


def deliver(values):
    return lax.all_to_all(
        values, ("blocks", "split", "inner"), split_axis=1, concat_axis=1, tiled=True
    )


def local(state, metrics, inv_volume, iblank, donor_cells, donor_fracs, receiver_cells):
    components, planes, columns, depth = state.shape
    cell_count = planes * columns * depth
    stencil = donor_cells[0]
    weights = corner_weights(donor_fracs[0])
    targets = receiver_cells[0]
    fringe = (
        jnp.zeros((cell_count,), jnp.bool_)
        .at[targets]
        .set(True, mode="drop")
        .reshape(planes, columns, depth)
    )
    update = jnp.logical_and(iblank == 1, jnp.logical_not(fringe))
    first_metric = metrics[0:3]
    normal_ext = extend_across(
        extended_2(first_metric, ((("split", "inner"), 1),), 1), first_metric
    )

    def fill_fringe(current):
        flattened = current.reshape(components, cell_count)
        values = jnp.sum(flattened[:, stencil] * weights[None], axis=1)
        arrived = deliver(values)
        return flattened.at[:, targets].set(arrived, mode="drop").reshape(current.shape)

    def advance(current):
        state_ext = extend_across(extended_2(current, ((("split", "inner"), 1),), 1), current)
        return current + TIME_STEP * residual_rate(
            current, state_ext, normal_ext, metrics, inv_volume
        )

    first_fill = fill_fringe(state)
    middle = jnp.where(update[None], advance(first_fill), first_fill)
    second_fill = fill_fringe(middle)
    return jnp.where(update[None], 0.5 * first_fill + 0.5 * advance(second_fill), second_fill)


def solution(mesh):
    return jax.shard_map(
        local,
        mesh=mesh,
        in_specs=(
            P(None, ("cases", "blocks", "split", "inner"), None, None),
            P(None, ("blocks", "split", "inner"), None, None),
            P(("blocks", "split", "inner"), None, None),
            P(("blocks", "split", "inner"), None, None),
            P(("blocks", "split", "inner"), None, None),
            P(("blocks", "split", "inner"), None, None),
            P(("blocks", "split", "inner"), None),
        ),
        out_specs=P(None, ("cases", "blocks", "split", "inner"), None, None),
        check_vma=False,
    )
```

profile of v0, /device:TPU:1, one launch (start us, length us, event | category | flops | bytes accessed | tf_op | source)
XLA Modules:
  0.0 89.0 jit_solution(3570651709687098703)
XLA Ops:
  0.0 0.9 fusion.241
  0.9 4.5 %collective-permute-start.1 = (f32[3,1,16,256]{3,2,1,0:T(8,128)S(1)}, f32[3,1,16,256]{3,2,1,0:T(8,128)S(1)}, u32[]{:S(2)}, u32[]{:S(2)}) collective-permute-start(f32[3,1,16,256]{3,2,1,0:T(8,128)S(1)} %get-tuple-element.71), channel_id=1, source_target_pairs={{0,1},{1,2},{2,3},{4,5},{5,6},{6,7},{8,9},{9,10},{10,11},{12,13},{... | collective-permute-start | bytes 147464 | tf_op jit(solution)/shard_map/ppermute | solution.py:18
  5.4 1.9 %collective-permute-start.2 = (f32[3,1,16,256]{3,2,1,0:T(8,128)S(1)}, f32[3,1,16,256]{3,2,1,0:T(8,128)S(1)}, u32[]{:S(2)}, u32[]{:S(2)}) collective-permute-start(f32[3,1,16,256]{3,2,1,0:T(8,128)S(1)} %get-tuple-element.72), channel_id=1, source_target_pairs={{1,0},{2,1},{3,2},{5,4},{6,5},{7,6},{9,8},{10,9},{11,10},{13,12},{... | collective-permute-start | bytes 147464 | tf_op jit(solution)/shard_map/ppermute | solution.py:20
  7.3 0.7 bitcast_multiply_fusion.37
  8.1 0.7 bitcast_multiply_fusion.36
  8.8 0.7 fusion.221
  9.5 3.5 %copy.138 = f32[5,2,16,256]{0,3,2,1:T(8,128)} copy(f32[5,2,16,256]{3,2,1,0:T(8,128)} %param.7) | data formatting | bytes 327680 | tf_op args[0]
  13.0 7.6 %gather_fusion = f32[2048,5]{1,0:T(8,128)S(1)} fusion(f32[5,8192]{0,1:T(8,128)} %bitcast.427, s32[2048]{0:T(1024)S(1)} %broadcast_clamp_fusion), kind=kCustom, calls=%fused_computation | custom fusion | bytes 90112 | tf_op jit(solution)/shard_map/gather | solution.py:125
  20.7 0.3 multiply_reduce_fusion.1
  21.0 0.8 copy.140
  21.8 6.5 %all-to-all-start = ((f32[5,16,16]{2,0,1:T(8,128)}), f32[5,16,16]{2,0,1:T(8,128)S(1)}, u32[]{:S(2)}, u32[]{:S(2)}) async-start(f32[5,16,16]{2,0,1:T(8,128)} %copy.140), calls=%async_computation | async-start | bytes 131072 | tf_op jit(solution)/shard_map/all_to_all | solution.py:100
  28.3 0.1 fusion.244
  28.4 1.5 %scatter_custom_fusion = pred[8192]{0:T(1024)(128)(4,1)S(1)} fusion(s32[256]{0:T(256)S(1)} %bitcast.440, pred[256]{0:T(512)(128)(4,1)S(1)} %broadcast.410, pred[]{:T(512)} %constant.16.clone.1), kind=kCustom, calls=%fused_computation.547 | custom fusion | bytes 8193 | tf_op jit(solution)/shard_map/scatter | solution.py:114
  30.1 4.2 %all-to-all-done = f32[5,16,16]{2,0,1:T(8,128)S(1)} async-done(((f32[5,16,16]{2,0,1:T(8,128)}), f32[5,16,16]{2,0,1:T(8,128)S(1)}, u32[]{:S(2)}, u32[]{:S(2)}) %all-to-all-start) | async-done | bytes 5152 | tf_op jit(solution)/shard_map/all_to_all | solution.py:100
  34.3 0.1 reshape.599
  34.4 0.1 copy.142
  34.6 5.2 %scatter_fusion = f32[5,8192]{0,1:T(8,128)} fusion(f32[5,8192]{0,1:T(8,128)} %bitcast.428, s32[256]{0:T(256)S(1)} %bitcast.441, f32[256,5]{1,0:T(8,128)S(1)} %copy.142), kind=kCustom, calls=%fused_computation.3 | custom fusion | bytes 16384 | tf_op jit(solution)/shard_map/scatter | solution.py:127
  39.8 2.9 %copy.175 = f32[5,2,16,256]{3,2,1,0:T(8,128)S(1)} copy(f32[5,2,16,256]{0,3,2,1:T(8,128)} %bitcast.429) | data formatting | bytes 327680 | tf_op jit(solution)/shard_map/reshape | solution.py:127
  42.7 0.1 fusion.250
  42.8 2.6 %collective-permute-start = (f32[5,1,16,256]{3,2,1,0:T(8,128)S(1)}, f32[5,1,16,256]{3,2,1,0:T(8,128)S(1)}, u32[]{:S(2)}, u32[]{:S(2)}) collective-permute-start(f32[5,1,16,256]{3,2,1,0:T(8,128)S(1)} %get-tuple-element.112), channel_id=1, source_target_pairs={{0,1},{1,2},{2,3},{4,5},{5,6},{6,7},{8,9},{9,10},{10,11},{12,13},{... | collective-permute-start | bytes 245768 | tf_op jit(solution)/shard_map/ppermute | solution.py:18
  45.4 1.9 %collective-permute-start.3 = (f32[5,1,16,256]{3,2,1,0:T(8,128)S(1)}, f32[5,1,16,256]{3,2,1,0:T(8,128)S(1)}, u32[]{:S(2)}, u32[]{:S(2)}) collective-permute-start(f32[5,1,16,256]{3,2,1,0:T(8,128)S(1)} %get-tuple-element.113), channel_id=1, source_target_pairs={{1,0},{2,1},{3,2},{5,4},{6,5},{7,6},{9,8},{10,9},{11,10},{13,12},{... | collective-permute-start | bytes 245768 | tf_op jit(solution)/shard_map/ppermute | solution.py:20
  47.3 0.1 fusion.231
  47.4 0.2 multiply_reduce_fusion.16
  47.6 0.1 fusion.196
  47.8 0.1 constant_dynamic-update-slice_fusion.26
  47.9 0.1 constant_dynamic-update-slice_fusion.25
  47.9 0.1 constant_dynamic-update-slice_fusion.21
  48.0 0.1 constant_dynamic-update-slice_fusion.20
  48.1 0.1 multiply_reduce_fusion.21
  48.3 0.1 fusion.205
  48.5 0.1 fusion.8
  48.7 0.1 fusion.17
  48.8 2.3 %collective-permute-done.3 = f32[5,1,16,256]{3,2,1,0:T(8,128)S(1)} collective-permute-done((f32[5,1,16,256]{3,2,1,0:T(8,128)S(1)}, f32[5,1,16,256]{3,2,1,0:T(8,128)S(1)}, u32[]{:S(2)}, u32[]{:S(2)}) %collective-permute-start.3) | collective-permute-done | bytes 81952 | tf_op jit(solution)/shard_map/ppermute | solution.py:20
  51.2 0.1 multiply_reduce_fusion.26
  51.3 0.1 fusion.214
  51.5 0.1 fusion.11
  51.6 0.1 add_select_fusion
  51.8 2.7 %copy.157 = f32[5,2,16,256]{0,3,2,1:T(8,128)} copy(f32[5,2,16,256]{3,2,1,0:T(8,128)S(1)} %add_select_fusion) | data formatting | bytes 327680 | tf_op jit(solution)/shard_map/jit(_where)/select_n | solution.py:136
  54.4 7.6 %gather_fusion.1 = f32[2048,5]{1,0:T(8,128)S(1)} fusion(f32[5,8192]{0,1:T(8,128)} %bitcast.430, s32[2048]{0:T(1024)S(1)} %broadcast_clamp_fusion), kind=kCustom, calls=%fused_computation.1 | custom fusion | bytes 90112 | tf_op jit(solution)/shard_map/gather | solution.py:125
  62.1 0.3 multiply_reduce_fusion
  62.4 0.2 copy.159
  62.6 8.3 %all_to_all.24 = f32[5,16,16]{2,0,1:T(8,128)S(1)} all-to-all(f32[5,16,16]{2,0,1:T(8,128)S(1)} %copy.159), channel_id=1, replica_groups=mesh['cases'=2,'blocks'=4,'split'=2,'inner'=2] {'blocks','split','inner'}, dimensions={1} | all-to-all | bytes 10240 | tf_op jit(solution)/shard_map/all_to_all | solution.py:100
  70.9 0.1 reshape.607
  71.0 0.1 copy.161
  71.1 5.2 %scatter_fusion.1 = f32[5,8192]{0,1:T(8,128)} fusion(f32[5,8192]{0,1:T(8,128)} %bitcast.431, s32[256]{0:T(256)S(1)} %bitcast.442, f32[256,5]{1,0:T(8,128)S(1)} %copy.161), kind=kCustom, calls=%fused_computation.4 | custom fusion | bytes 16384 | tf_op jit(solution)/shard_map/scatter | solution.py:127
  76.3 2.9 %copy.174 = f32[5,2,16,256]{3,2,1,0:T(8,128)S(1)} copy(f32[5,2,16,256]{0,3,2,1:T(8,128)} %bitcast.432) | data formatting | bytes 327680 | tf_op jit(solution)/shard_map/reshape | solution.py:127
  79.3 0.1 fusion.247
  79.4 2.6 %collective-permute-start.4 = (f32[5,1,16,256]{3,2,1,0:T(8,128)S(1)}, f32[5,1,16,256]{3,2,1,0:T(8,128)S(1)}, u32[]{:S(2)}, u32[]{:S(2)}) collective-permute-start(f32[5,1,16,256]{3,2,1,0:T(8,128)S(1)} %get-tuple-element.92), channel_id=1, source_target_pairs={{0,1},{1,2},{2,3},{4,5},{5,6},{6,7},{8,9},{9,10},{10,11},{12,13},{... | collective-permute-start | bytes 245768 | tf_op jit(solution)/shard_map/ppermute | solution.py:18
  82.0 1.9 %collective-permute-start.5 = (f32[5,1,16,256]{3,2,1,0:T(8,128)S(1)}, f32[5,1,16,256]{3,2,1,0:T(8,128)S(1)}, u32[]{:S(2)}, u32[]{:S(2)}) collective-permute-start(f32[5,1,16,256]{3,2,1,0:T(8,128)S(1)} %get-tuple-element.93), channel_id=1, source_target_pairs={{1,0},{2,1},{3,2},{5,4},{6,5},{7,6},{9,8},{10,9},{11,10},{13,12},{... | collective-permute-start | bytes 245768 | tf_op jit(solution)/shard_map/ppermute | solution.py:20
  83.9 0.1 fusion.237
  84.0 0.2 multiply_reduce_fusion.3
  84.1 0.1 fusion.180
  84.3 0.1 constant_dynamic-update-slice_fusion.56
  84.4 0.1 constant_dynamic-update-slice_fusion.55
  84.5 0.1 constant_dynamic-update-slice_fusion.51
  84.6 0.1 constant_dynamic-update-slice_fusion.50
  84.7 0.1 multiply_reduce_fusion.7
  84.8 0.1 fusion.185
  85.0 0.1 fusion.2
  85.2 0.1 fusion.14
  85.3 2.5 %collective-permute-done.5 = f32[5,1,16,256]{3,2,1,0:T(8,128)S(1)} collective-permute-done((f32[5,1,16,256]{3,2,1,0:T(8,128)S(1)}, f32[5,1,16,256]{3,2,1,0:T(8,128)S(1)}, u32[]{:S(2)}, u32[]{:S(2)}) %collective-permute-start.5) | collective-permute-done | bytes 81952 | tf_op jit(solution)/shard_map/ppermute | solution.py:20
  87.8 0.1 fusion.190
  88.1 0.1 fusion.5
  88.2 0.8 fusion.24
  (66 shorter events, 1.1 us)
Async XLA Ops:
  0.0 28.3 %copy-start = (f32[9,2,16,256]{3,2,1,0:T(8,128)S(1)}, f32[9,2,16,256]{3,2,1,0:T(8,128)}, u32[]{:S(2)}) copy-start(f32[9,2,16,256]{3,2,1,0:T(8,128)} %param.8) | copy-start | bytes 884740
  0.0 28.4 %copy-start.3 = (s32[1,256]{1,0:T(1,128)S(1)}, s32[1,256]{1,0:T(1,128)}, u32[]{:S(2)}) copy-start(s32[1,256]{1,0:T(1,128)} %param.13) | copy-start | bytes 3076
  0.0 30.0 %copy-start.1 = (s32[2,16,256]{2,1,0:T(8,128)S(1)}, s32[2,16,256]{2,1,0:T(8,128)}, u32[]{:S(2)}) copy-start(s32[2,16,256]{2,1,0:T(8,128)} %param.10) | copy-start | bytes 98308
  0.0 30.1 %copy-start.2 = (f32[2,16,256]{2,1,0:T(8,128)S(1)}, f32[2,16,256]{2,1,0:T(8,128)}, u32[]{:S(2)}) copy-start(f32[2,16,256]{2,1,0:T(8,128)} %param.9) | copy-start | bytes 98308
  0.9 47.8 %collective-permute-start.1 = (f32[3,1,16,256]{3,2,1,0:T(8,128)S(1)}, f32[3,1,16,256]{3,2,1,0:T(8,128)S(1)}, u32[]{:S(2)}, u32[]{:S(2)}) collective-permute-start(f32[3,1,16,256]{3,2,1,0:T(8,128)S(1)} %get-tuple-element.71), channel_id=1, source_target_pairs={{0,1},{1,2},{2,3},{4,5},{5,6},{6,7},{8,9},{9,10},{10,11},{12,13},{... | collective-permute-start | bytes 147464 | tf_op jit(solution)/shard_map/ppermute | solution.py:18
  5.4 43.4 %collective-permute-start.2 = (f32[3,1,16,256]{3,2,1,0:T(8,128)S(1)}, f32[3,1,16,256]{3,2,1,0:T(8,128)S(1)}, u32[]{:S(2)}, u32[]{:S(2)}) collective-permute-start(f32[3,1,16,256]{3,2,1,0:T(8,128)S(1)} %get-tuple-element.72), channel_id=1, source_target_pairs={{1,0},{2,1},{3,2},{5,4},{6,5},{7,6},{9,8},{10,9},{11,10},{13,12},{... | collective-permute-start | bytes 147464 | tf_op jit(solution)/shard_map/ppermute | solution.py:20
  21.8 12.5 %all-to-all-start = ((f32[5,16,16]{2,0,1:T(8,128)}), f32[5,16,16]{2,0,1:T(8,128)S(1)}, u32[]{:S(2)}, u32[]{:S(2)}) async-start(f32[5,16,16]{2,0,1:T(8,128)} %copy.140), calls=%async_computation | async-start | bytes 131072 | tf_op jit(solution)/shard_map/all_to_all | solution.py:100
  42.8 6.0 %collective-permute-start = (f32[5,1,16,256]{3,2,1,0:T(8,128)S(1)}, f32[5,1,16,256]{3,2,1,0:T(8,128)S(1)}, u32[]{:S(2)}, u32[]{:S(2)}) collective-permute-start(f32[5,1,16,256]{3,2,1,0:T(8,128)S(1)} %get-tuple-element.112), channel_id=1, source_target_pairs={{0,1},{1,2},{2,3},{4,5},{5,6},{6,7},{8,9},{9,10},{10,11},{12,13},{... | collective-permute-start | bytes 245768 | tf_op jit(solution)/shard_map/ppermute | solution.py:18
  45.4 5.8 %collective-permute-start.3 = (f32[5,1,16,256]{3,2,1,0:T(8,128)S(1)}, f32[5,1,16,256]{3,2,1,0:T(8,128)S(1)}, u32[]{:S(2)}, u32[]{:S(2)}) collective-permute-start(f32[5,1,16,256]{3,2,1,0:T(8,128)S(1)} %get-tuple-element.113), channel_id=1, source_target_pairs={{1,0},{2,1},{3,2},{5,4},{6,5},{7,6},{9,8},{10,9},{11,10},{13,12},{... | collective-permute-start | bytes 245768 | tf_op jit(solution)/shard_map/ppermute | solution.py:20
  79.4 5.9 %collective-permute-start.4 = (f32[5,1,16,256]{3,2,1,0:T(8,128)S(1)}, f32[5,1,16,256]{3,2,1,0:T(8,128)S(1)}, u32[]{:S(2)}, u32[]{:S(2)}) collective-permute-start(f32[5,1,16,256]{3,2,1,0:T(8,128)S(1)} %get-tuple-element.92), channel_id=1, source_target_pairs={{0,1},{1,2},{2,3},{4,5},{5,6},{6,7},{8,9},{9,10},{10,11},{12,13},{... | collective-permute-start | bytes 245768 | tf_op jit(solution)/shard_map/ppermute | solution.py:18
  82.0 5.8 %collective-permute-start.5 = (f32[5,1,16,256]{3,2,1,0:T(8,128)S(1)}, f32[5,1,16,256]{3,2,1,0:T(8,128)S(1)}, u32[]{:S(2)}, u32[]{:S(2)}) collective-permute-start(f32[5,1,16,256]{3,2,1,0:T(8,128)S(1)} %get-tuple-element.93), channel_id=1, source_target_pairs={{1,0},{2,1},{3,2},{5,4},{6,5},{7,6},{9,8},{10,9},{11,10},{13,12},{... | collective-permute-start | bytes 245768 | tf_op jit(solution)/shard_map/ppermute | solution.py:20
where the time goes:
time: 89.6 us; the launch traced here: 89 us
  local copies, waits for them, and re-layouts  41.8 us (47%)
  starting transfers between devices  21.9 us (24%)
  waiting for transfers between devices  9.03 us (10%)
  blocking collectives  8.33 us (9%)
  other arithmetic  7.25 us (8%)
    gather x2, local copies, waits for them, and re-layouts, fill_fringe(): values = jnp.sum(flattened[:, stencil] * weights[None], axis=1)  15.3 us
    scatter x2, local copies, waits for them, and re-layouts, fill_fringe(): flattened.at[:, targets].set(arrived, mode='drop').reshape(current.shape)  10.4 us
    ppermute x3, starting transfers between devices, extended_2(): lax.ppermute(tail, axis, [(i, (i + 1) % count) for i in range(ends)])  9.68 us
    all_to_all x1, blocking collectives, deliver(): lax.all_to_all(values, ('blocks', 'split', 'inner'), split_axis=1, concat...  8.33 us
    all_to_all x1, starting transfers between devices, deliver(): lax.all_to_all(values, ('blocks', 'split', 'inner'), split_axis=1, concat...  6.45 us
    ppermute x3, starting transfers between devices, extended_2(): lax.ppermute(head, axis, [((i + 1) % count, i) for i in range(ends)])  5.76 us
    reshape x2, local copies, waits for them, and re-layouts, fill_fringe(): flattened.at[:, targets].set(arrived, mode='drop').reshape(current.shape)  5.74 us
    ppermute x3, waiting for transfers between devices, extended_2(): lax.ppermute(head, axis, [((i + 1) % count, i) for i in range(ends)])  4.8 us
  transfers between devices with their start and end apart: 7, of which 3 were waited for; matrix products, arithmetic and copies ran while one was open for 31% of the time, Pallas kernels for 0%

commit v1 on v0

v1 whole, which is shorter than its diff:
```python
import functools

import jax
import jax.numpy as jnp
from jax import lax
from jax.experimental import pallas as pl
from jax.experimental.pallas import tpu as pltpu
from jax.sharding import PartitionSpec as P

HEAT_RATIO = 1.4
TIME_STEP = 0.08
GROUP = ("blocks", "split", "inner")
LANES = 128
MESH = pl.DeviceIdType.MESH


def split3(x):
    high = x.astype(jnp.bfloat16)
    rest = x - high.astype(jnp.float32)
    middle = rest.astype(jnp.bfloat16)
    low = (rest - middle.astype(jnp.float32)).astype(jnp.bfloat16)
    return high, middle, low


def primitive(u):
    density, m0, m1, m2, energy = u
    inverse = 1.0 / density
    pressure = (HEAT_RATIO - 1.0) * (energy - 0.5 * (m0 * m0 + m1 * m1 + m2 * m2) * inverse)
    sound = jnp.sqrt(HEAT_RATIO * pressure * inverse)
    return (density, m0, m1, m2, energy, inverse, pressure, sound)


def face(left, right, normal):
    n0, n1, n2, length = normal
    dl, al, bl, cl, el, il, pl_, sl = left
    dr, ar, br, cr, er, ir, pr, sr = right
    flow_l = al * n0 + bl * n1 + cl * n2
    flow_r = ar * n0 + br * n1 + cr * n2
    wl = flow_l * il
    wr = flow_r * ir
    radius = jnp.maximum(jnp.abs(wl) + sl * length, jnp.abs(wr) + sr * length)
    both = pl_ + pr
    return (
        flow_l + flow_r - radius * (dr - dl),
        al * wl + ar * wr + both * n0 - radius * (ar - al),
        bl * wl + br * wr + both * n1 - radius * (br - bl),
        cl * wl + cr * wr + both * n2 - radius * (cr - cl),
        (el + pl_) * wl + (er + pr) * wr - radius * (er - el),
    )


def twice_flux(cell, normal):
    n0, n1, n2 = (2.0 * n for n in normal)
    _, a, b, c, e, inverse, p, _ = cell
    flow = a * n0 + b * n1 + c * n2
    w = flow * inverse
    return (flow, a * w + p * n0, b * w + p * n1, c * w + p * n2, (e + p) * w)


def next_along(x, axis):
    size = x.shape[axis]
    index = lax.broadcasted_iota(jnp.int32, x.shape, axis)
    return jnp.where(index == size - 1, x, pltpu.roll(x, size - 1, axis))


def averaged(first, second):
    n = tuple(0.5 * (a + b) for a, b in zip(first, second))
    return n + (jnp.sqrt(n[0] * n[0] + n[1] * n[1] + n[2] * n[2]),)


def difference_along(cell, upper_normal, own_normal, axis):
    upper = face(cell, tuple(next_along(x, axis) for x in cell), upper_normal)
    span = 8 if axis == 0 else LANES
    cut = functools.partial(lax.slice_in_dim, start_index=0, limit_index=span, axis=axis)
    ghost = twice_flux(tuple(cut(x) for x in cell), tuple(cut(x) for x in own_normal))
    out = []
    for value, edge in zip(upper, ghost):
        lower = pltpu.roll(value, 1, axis)
        index = lax.broadcasted_iota(jnp.int32, edge.shape, axis)
        first = jnp.where(index == 0, edge, cut(lower))
        rest = lax.slice_in_dim(lower, span, lower.shape[axis], axis=axis)
        out.append(value - jnp.concatenate([first, rest], axis=axis))
    return out


def kernel(
    sizes,
    state_hbm, metrics_hbm, volume_hbm, blank_hbm, cells_hbm, fracs_hbm, targets_hbm,
    out_ref,
    state, metrics, volume, blank, cells, fracs, targets,
    hot, spread, send, recv, halo, halo_metrics, halo_targets, filled, middle, normals, marks,
    load_sem, send_sem, recv_sem, halo_send, halo_recv, once_send, once_recv,
):
    blocks, splits, inners = sizes
    n = blocks * splits * inners
    line = splits * inners
    nvar, planes, columns, depth = state.shape
    slots = targets.shape[1]
    cap = slots // n
    per = LANES // cap
    tiles = slots // LANES

    place = lax.axis_index("split") * inners + lax.axis_index("inner")
    me = lax.axis_index("blocks") * line + place
    has_left = place > 0
    has_right = place < line - 1

    def peer(r):
        return {"blocks": r // line, "split": (r // inners) % splits, "inner": r % inners}

    def beside(step):
        q = place + step
        return {"split": q // inners, "inner": q % inners}

    loads = [
        pltpu.make_async_copy(src, dst, load_sem.at[i])
        for i, (src, dst) in enumerate(
            (
                (cells_hbm, cells), (fracs_hbm, fracs), (state_hbm, state), (targets_hbm, targets),
                (metrics_hbm, metrics), (volume_hbm, volume), (blank_hbm, blank),
            )
        )
    ]
    for load in loads:
        load.start()
    barrier = pltpu.get_barrier_semaphore()
    for d in range(1, n):
        pl.semaphore_signal(
            barrier, inc=1, device_id=peer(lax.rem(me + d, n)), device_id_type=MESH
        )

    def row_of(index, length):
        return lax.broadcasted_iota(jnp.int32, (length, slots), 0) == index

    def one_hot(index, length):
        return jnp.where(row_of(index, length), 1.0, 0.0)

    loads[0].wait()
    loads[1].wait()
    corner = cells[0, 0:1, :]
    k0 = corner % depth
    j0 = (corner // depth) % columns
    i0 = corner // (depth * columns)
    f0, f1, f2 = (fracs[0, g : g + 1, :] for g in range(3))
    hot[:, 0:slots] = one_hot(k0, depth).astype(jnp.bfloat16)
    hot[:, slots : 2 * slots] = one_hot(k0 + 1, depth).astype(jnp.bfloat16)
    weight_j = one_hot(j0, columns) * (1.0 - f1) + one_hot(j0 + 1, columns) * f1
    weight_i = [
        jnp.where(i0 == i, 1.0 - f0, 0.0) + jnp.where(i0 + 1 == i, f0, 0.0)
        for i in range(planes)
    ]
    for i in range(planes):
        marks[i] = weight_j * weight_i[i]

    def gather(source, step):
        rows = nvar * planes * columns
        flat = source[...].reshape(rows, depth)
        parts = split3(flat)
        picked = sum(
            jnp.dot(part, hot[...], preferred_element_type=jnp.float32) for part in parts[::-1]
        )
        along = picked[:, 0:slots] * (1.0 - f2) + picked[:, slots : 2 * slots] * f2
        along = along.reshape(nvar, planes, columns, slots)
        for v in range(nvar):
            total = along[v, 0] * marks[0]
            for i in range(1, planes):
                total = total + along[v, i] * marks[i]
            row = jnp.sum(total, axis=0, keepdims=True)
            for h in range(tiles):
                send[step, h, v : v + 1, :] = row[:, h * LANES : (h + 1) * LANES]

    def exchange(step):
        copies = []
        for d in range(1, n):
            r = lax.rem(me + d, n)
            copies.append(
                pltpu.make_async_remote_copy(
                    src_ref=send.at[step, r // per],
                    dst_ref=recv.at[step, me],
                    send_sem=send_sem.at[step],
                    recv_sem=recv_sem.at[step],
                    device_id=peer(r),
                    device_id_type=MESH,
                )
            )
        for copy in copies:
            copy.start()
        recv[step, me] = send[step, me // per]

    def drain(step, sem):
        pltpu.make_async_copy(
            recv.at[step, pl.ds(0, n - 1)], recv.at[step, pl.ds(0, n - 1)], sem.at[step]
        ).wait()

    def halo_copies(source, step):
        return [
            pltpu.make_async_remote_copy(
                src_ref=source.at[:, 0 if side else planes - 1],
                dst_ref=halo.at[step, side],
                send_sem=halo_send.at[step, side],
                recv_sem=halo_recv.at[step, side],
                device_id=beside(-1 if side else 1),
                device_id_type=MESH,
            )
            for side in range(2)
        ]

    def once_copies():
        out = []
        for side in range(2):
            for item, (src, dst) in enumerate(
                (
                    (targets, halo_targets.at[side]),
                    (metrics.at[pl.ds(0, 3), 0 if side else planes - 1], halo_metrics.at[side]),
                )
            ):
                out.append(
                    pltpu.make_async_remote_copy(
                        src_ref=src,
                        dst_ref=dst,
                        send_sem=once_send.at[side, item],
                        recv_sem=once_recv.at[side, item],
                        device_id=beside(-1 if side else 1),
                        device_id_type=MESH,
                    )
                )
        return out[:2], out[2:]

    def both_sides(pairs, act):
        for side, sends in ((0, has_right), (1, has_left)):

            @pl.when(sends if act in ("start", "wait_send") else (has_left, has_right)[side])
            def _():
                for copy in pairs[side]:
                    getattr(copy, act)()

    loads[2].wait()
    gather(state, 0)
    for load in loads[3:5]:
        load.wait()
    pl.semaphore_wait(barrier, n - 1)
    exchange(0)
    once = once_copies()
    halo_0 = [[copy] for copy in halo_copies(state, 0)]
    both_sides(halo_0, "start")
    both_sides(once, "start")

    for i in range(planes):
        for g in (1, 2):
            own = tuple(metrics[3 * g + x, i] for x in range(3))
            mean = averaged(own, tuple(next_along(x, g - 1) for x in own))
            for x in range(4):
                normals[g, i, x] = mean[x]

    def spread_of(index, cell):
        spread[index] = one_hot(cell % depth, depth).astype(jnp.bfloat16)

    spread_of(0, targets[...])
    for load in loads[5:]:
        load.wait()
    both_sides(once, "wait_recv")
    for side in range(2):
        spread_of(1 + side, halo_targets[side])
    place_rows = [
        targets[...] // depth,
        halo_targets[0] // depth - (planes - 1) * columns,
        halo_targets[1] // depth,
    ]
    rows_of = [planes * columns, columns, columns]
    nt = (((1,), (1,)), ((), ()))
    fringe = []
    for t in range(3):
        found = lax.dot_general(
            one_hot(place_rows[t], rows_of[t]).astype(jnp.bfloat16), spread[t], nt,
            preferred_element_type=jnp.float32,
        )
        fringe.append(found > 0.5)

    first = [metrics[x, 0] for x in range(3)]
    last = [metrics[x, planes - 1] for x in range(3)]
    line_normals = [
        tuple(jnp.where(has_left, halo_metrics[0, x], first[x]) for x in range(3))
    ]
    for i in range(planes):
        line_normals.append(tuple(metrics[x, i] for x in range(3)))
    line_normals.append(
        tuple(jnp.where(has_right, halo_metrics[1, x], last[x]) for x in range(3))
    )
    for i in range(planes + 1):
        mean = averaged(line_normals[i], line_normals[i + 1])
        for x in range(4):
            normals[0, i, x] = mean[x]

    segment = lax.broadcasted_iota(jnp.int32, (8, LANES), 1) // cap

    def arrived(step):
        whole = [[], [], []]
        for h in range(tiles):
            sums = [jnp.zeros((8, LANES), jnp.float32)] * 3
            for o in range(h * per, (h + 1) * per):
                tile = pltpu.roll(recv[step, o], lax.rem(o - me + n * per, per) * cap, 1)
                for t, shift in enumerate((0, -1, 1)):
                    sums[t] = jnp.where(segment == (o + shift) % per, tile, sums[t])
            whole[0].append(sums[0])
            whole[1].append(pltpu.roll(sums[1], cap, 1))
            whole[2].append(pltpu.roll(sums[2], LANES - cap, 1))
        return [jnp.concatenate(w, axis=1) for w in whole]

    def fill(step, t, values, current):
        mine = row_of(place_rows[t], rows_of[t])
        parts = []
        for part in split3(values):
            wide = part.astype(jnp.float32)
            parts.append(
                jnp.concatenate(
                    [jnp.where(mine, wide[v : v + 1, :], 0.0) for v in range(nvar)], axis=0
                ).astype(jnp.bfloat16)
            )
        placed = sum(
            lax.dot_general(part, spread[t], nt, preferred_element_type=jnp.float32)
            for part in parts[::-1]
        )
        out = []
        for i, plane in enumerate(current):
            at = slice(i * columns, (i + 1) * columns)
            out.append(
                [
                    jnp.where(
                        fringe[t][at],
                        placed[v * rows_of[t] + i * columns : v * rows_of[t] + (i + 1) * columns],
                        plane[v],
                    )
                    for v in range(nvar)
                ]
            )
        return out

    def planes_of(ref):
        return [[ref[v, i] for v in range(nvar)] for i in range(planes)]

    def section(step, source, halo_pairs):
        drain(step, recv_sem)
        values = arrived(step)
        own = fill(step, 0, values[0], planes_of(source))
        for i in range(planes):
            for v in range(nvar):
                filled[step, v, i] = own[i][v]
        both_sides(halo_pairs, "wait_recv")
        left = fill(step, 1, values[1], [[halo[step, 0, v] for v in range(nvar)]])[0]
        right = fill(step, 2, values[2], [[halo[step, 1, v] for v in range(nvar)]])[0]
        left = [jnp.where(has_left, a, b) for a, b in zip(left, own[0])]
        right = [jnp.where(has_right, a, b) for a, b in zip(right, own[planes - 1])]
        cell = [primitive(u) for u in [left] + own + [right]]
        faces = [
            face(cell[i], cell[i + 1], tuple(normals[0, i, x] for x in range(4)))
            for i in range(planes + 1)
        ]
        stepped = []
        for i in range(planes):
            total = [b - a for a, b in zip(faces[i], faces[i + 1])]
            for g in (1, 2):
                more = difference_along(
                    cell[i + 1],
                    tuple(normals[g, i, x] for x in range(4)),
                    tuple(metrics[3 * g + x, i] for x in range(3)),
                    g - 1,
                )
                total = [a + b for a, b in zip(total, more)]
            factor = (-0.5 * TIME_STEP) * volume[i]
            update = jnp.logical_and(
                blank[i] == 1, jnp.logical_not(fringe[0][i * columns : (i + 1) * columns])
            )
            stepped.append((update, [factor * x for x in total]))
        return stepped

    for i, (update, change) in enumerate(section(0, state, halo_0)):
        for v in range(nvar):
            middle[v, i] = filled[0, v, i] + jnp.where(update, change[v], 0.0)
    halo_1 = [[copy] for copy in halo_copies(middle, 1)]
    both_sides(halo_1, "start")
    gather(middle, 1)
    exchange(1)
    for i, (update, change) in enumerate(section(1, middle, halo_1)):
        for v in range(nvar):
            end = filled[1, v, i]
            out_ref[v, i] = jnp.where(
                update, 0.5 * filled[0, v, i] + 0.5 * (end + change[v]), end
            )
    for step in range(2):
        drain(step, send_sem)
    for pairs in (halo_0, halo_1, once):
        both_sides(pairs, "wait_send")


def local(sizes, state, metrics, inv_volume, iblank, donor_cells, donor_fracs, receiver_cells):
    nvar, planes, columns, depth = state.shape
    slots = receiver_cells.shape[1]
    n = sizes[0] * sizes[1] * sizes[2]
    tiles = slots // LANES
    f32, bf16, i32 = jnp.float32, jnp.bfloat16, jnp.int32
    dma = pltpu.SemaphoreType.DMA
    return pl.pallas_call(
        functools.partial(kernel, sizes),
        out_shape=jax.ShapeDtypeStruct(state.shape, f32),
        in_specs=[pl.BlockSpec(memory_space=pl.ANY)] * 7,
        out_specs=pl.BlockSpec(memory_space=pltpu.VMEM),
        scratch_shapes=[
            pltpu.VMEM(state.shape, f32),
            pltpu.VMEM(metrics.shape, f32),
            pltpu.VMEM(inv_volume.shape, f32),
            pltpu.VMEM(iblank.shape, i32),
            pltpu.VMEM(donor_cells.shape, i32),
            pltpu.VMEM(donor_fracs.shape, f32),
            pltpu.VMEM(receiver_cells.shape, i32),
            pltpu.VMEM((depth, 2 * slots), bf16),
            pltpu.VMEM((3, depth, slots), bf16),
            pltpu.VMEM((2, tiles, 8, LANES), f32),
            pltpu.VMEM((2, n, 8, LANES), f32),
            pltpu.VMEM((2, 2, nvar, columns, depth), f32),
            pltpu.VMEM((2, 3, columns, depth), f32),
            pltpu.VMEM((2, 1, slots), i32),
            pltpu.VMEM((2,) + state.shape, f32),
            pltpu.VMEM(state.shape, f32),
            pltpu.VMEM((3, planes + 1, 4, columns, depth), f32),
            pltpu.VMEM((planes, columns, slots), f32),
            dma((7,)),
            dma((2,)),
            dma((2,)),
            dma((2, 2)),
            dma((2, 2)),
            dma((2, 2)),
            dma((2, 2)),
        ],
        compiler_params=pltpu.CompilerParams(
            collective_id=0, has_side_effects=True, vmem_limit_bytes=40 * 1024 * 1024
        ),
    )(state, metrics, inv_volume, iblank, donor_cells, donor_fracs, receiver_cells)


def solution(mesh):
    sizes = tuple(mesh.shape[axis] for axis in GROUP)
    return jax.shard_map(
        functools.partial(local, sizes),
        mesh=mesh,
        in_specs=(
            P(None, ("cases", "blocks", "split", "inner"), None, None),
            P(None, ("blocks", "split", "inner"), None, None),
            P(("blocks", "split", "inner"), None, None),
            P(("blocks", "split", "inner"), None, None),
            P(("blocks", "split", "inner"), None, None),
            P(("blocks", "split", "inner"), None, None),
            P(("blocks", "split", "inner"), None),
        ),
        out_specs=P(None, ("cases", "blocks", "split", "inner"), None, None),
        check_vma=False,
    )
```

time: 89.6 us -> 23.2 us (0.26)
  the two profiles are of different devices: /device:TPU:1 before, /device:TPU:0 now
where the time goes in v1:
time: 23.2 us; the launch traced here: 22.9 us
  Pallas kernels  17.4 us (75%)
  local copies, waits for them, and re-layouts  5.46 us (24%)
    pallas_call x1, Pallas kernels, local(): pl.pallas_call(functools.partial(kernel, sizes), out_shape=jax.ShapeDtype...  17.4 us
    unnamed x14, local copies, waits for them, and re-layouts  5.46 us

profile of v1, /device:TPU:0, one launch (start us, length us, event | category | flops | bytes accessed | tf_op | source)
XLA Modules:
  0.0 22.9 jit_solution(5764598333567561185)
XLA Ops:
  0.0 0.0 copy-start.5
  0.0 0.7 %copy.8.fracs_hbm = f32[1,3,256]{2,1,0:T(4,128)S(1)} copy(f32[1,3,256]{2,0,1:T(1,128)} %param.12) | data formatting | bytes 6144 | tf_op args[5]
  0.7 0.0 copy-done.5
  0.7 0.0 copy-start
  0.7 1.0 %copy-done = f32[9,2,16,256]{3,2,1,0:T(8,128)S(1)} copy-done((f32[9,2,16,256]{3,2,1,0:T(8,128)S(1)}, f32[9,2,16,256]{3,2,1,0:T(8,128)}, u32[]{:S(2)}) %copy-start) | copy-done | bytes 294936
  1.7 0.0 copy-start.1
  1.7 0.9 %copy-done.1 = f32[5,2,16,256]{3,2,1,0:T(8,128)S(1)} copy-done((f32[5,2,16,256]{3,2,1,0:T(8,128)S(1)}, f32[5,2,16,256]{3,2,1,0:T(8,128)}, u32[]{:S(2)}) %copy-start.1) | copy-done | bytes 163864
  2.6 0.0 copy-start.2
  2.6 0.8 %copy-done.2 = f32[2,16,256]{2,1,0:T(8,128)S(1)} copy-done((f32[2,16,256]{2,1,0:T(8,128)S(1)}, f32[2,16,256]{2,1,0:T(8,128)}, u32[]{:S(2)}) %copy-start.2) | copy-done | bytes 32792
  3.3 0.0 copy-start.3
  3.3 0.8 %copy-done.3 = s32[2,16,256]{2,1,0:T(8,128)S(1)} copy-done((s32[2,16,256]{2,1,0:T(8,128)S(1)}, s32[2,16,256]{2,1,0:T(8,128)}, u32[]{:S(2)}) %copy-start.3) | copy-done | bytes 32792
  4.1 0.0 copy-start.4
  4.1 0.7 %copy-done.4 = s32[1,8,256]{2,1,0:T(8,128)S(1)} copy-done((s32[1,8,256]{2,1,0:T(8,128)S(1)}, s32[1,8,256]{2,1,0:T(8,128)}, u32[]{:S(2)}) %copy-start.4) | copy-done | bytes 8216
  4.8 17.4 %shard_map.73 = f32[5,2,16,256]{3,2,1,0:T(8,128)S(1)} custom-call(f32[5,2,16,256]{3,2,1,0:T(8,128)S(1)} %copy-done.1, f32[9,2,16,256]{3,2,1,0:T(8,128)S(1)} %copy-done, f32[2,16,256]{2,1,0:T(8,128)S(1)} %copy-done.2, s32[2,16,256]{2,1,0:T(8,128)S(1)} %copy-done.3, s32[1,8,256]{2,1,0:T(8,128)S(1)} %copy-done.4, f32[1,3,256]{2,1,0:T(4,128)S(1)} %copy.8.fracs_hbm, ...), custom_call_target="tpu_custom_call" | custom-call | tf_op jit(solution)/shard_map/pallas_call | solution.py:402
  22.2 0.7 %copy.10 = f32[5,2,16,256]{3,2,1,0:T(8,128)} copy(f32[5,2,16,256]{3,2,1,0:T(8,128)S(1)} %shard_map.73) | data formatting | bytes 327680
Async XLA Ops:
  0.0 0.7 %copy-start.5 = (s32[1,256]{1,0:T(1,128)S(1)}, s32[1,256]{1,0:T(1,128)}, u32[]{:S(2)}) copy-start(s32[1,256]{1,0:T(1,128)} %targets_hbm.1) | copy-start | bytes 3076
  0.7 1.0 %copy-start = (f32[9,2,16,256]{3,2,1,0:T(8,128)S(1)}, f32[9,2,16,256]{3,2,1,0:T(8,128)}, u32[]{:S(2)}) copy-start(f32[9,2,16,256]{3,2,1,0:T(8,128)} %metrics_hbm.1) | copy-start | bytes 884740
  1.7 0.9 %copy-start.1 = (f32[5,2,16,256]{3,2,1,0:T(8,128)S(1)}, f32[5,2,16,256]{3,2,1,0:T(8,128)}, u32[]{:S(2)}) copy-start(f32[5,2,16,256]{3,2,1,0:T(8,128)} %state_hbm.1) | copy-start | bytes 491524
  2.6 0.8 %copy-start.2 = (f32[2,16,256]{2,1,0:T(8,128)S(1)}, f32[2,16,256]{2,1,0:T(8,128)}, u32[]{:S(2)}) copy-start(f32[2,16,256]{2,1,0:T(8,128)} %volume_hbm.1) | copy-start | bytes 98308
  3.3 0.8 %copy-start.3 = (s32[2,16,256]{2,1,0:T(8,128)S(1)}, s32[2,16,256]{2,1,0:T(8,128)}, u32[]{:S(2)}) copy-start(s32[2,16,256]{2,1,0:T(8,128)} %blank_hbm.1) | copy-start | bytes 98308
  4.1 0.7 %copy-start.4 = (s32[1,8,256]{2,1,0:T(8,128)S(1)}, s32[1,8,256]{2,1,0:T(8,128)}, u32[]{:S(2)}) copy-start(s32[1,8,256]{2,1,0:T(8,128)} %cells_hbm.1) | copy-start | bytes 24580

commit v2 on v1

--- a/solution.py
+++ b/solution.py
@@ -141,7 +141,7 @@
     k0 = corner % depth
     j0 = (corner // depth) % columns
     i0 = corner // (depth * columns)
-    f0, f1, f2 = (fracs[0, g : g + 1, :] for g in range(3))
+    f0, f1, f2 = (fracs[g] for g in range(3))
     hot[:, 0:slots] = one_hot(k0, depth).astype(jnp.bfloat16)
     hot[:, slots : 2 * slots] = one_hot(k0 + 1, depth).astype(jnp.bfloat16)
     weight_j = one_hot(j0, columns) * (1.0 - f1) + one_hot(j0 + 1, columns) * f1
@@ -402,7 +402,7 @@
     return pl.pallas_call(
         functools.partial(kernel, sizes),
         out_shape=jax.ShapeDtypeStruct(state.shape, f32),
-        in_specs=[pl.BlockSpec(memory_space=pl.ANY)] * 7,
+        in_specs=[pl.BlockSpec(memory_space=pltpu.HBM)] * 7,
         out_specs=pl.BlockSpec(memory_space=pltpu.VMEM),
         scratch_shapes=[
             pltpu.VMEM(state.shape, f32),
@@ -410,7 +410,7 @@
             pltpu.VMEM(inv_volume.shape, f32),
             pltpu.VMEM(iblank.shape, i32),
             pltpu.VMEM(donor_cells.shape, i32),
-            pltpu.VMEM(donor_fracs.shape, f32),
+            pltpu.VMEM((3, 1, slots), f32),
             pltpu.VMEM(receiver_cells.shape, i32),
             pltpu.VMEM((depth, 2 * slots), bf16),
             pltpu.VMEM((3, depth, slots), bf16),
@@ -434,7 +434,15 @@
         compiler_params=pltpu.CompilerParams(
             collective_id=0, has_side_effects=True, vmem_limit_bytes=40 * 1024 * 1024
         ),
-    )(state, metrics, inv_volume, iblank, donor_cells, donor_fracs, receiver_cells)
+    )(
+        *(
+            pltpu.with_memory_space_constraint(x, pltpu.HBM)
+            for x in (
+                state, metrics, inv_volume, iblank, donor_cells,
+                donor_fracs.reshape(3, 1, slots), receiver_cells,
+            )
+        )
+    )
 
 
 def solution(mesh):

time: 23.2 us -> 17.9 us (0.77)
  local copies, waits for them, and re-layouts: 5.46 us -> 0.67 us
  Pallas kernels: 17.4 us -> 17 us
    unnamed x14 -> x1, local copies, waits for them, and re-layouts: 5.46 us -> 0.67 us
    pallas_call x1, Pallas kernels: 17.4 us -> 17 us  [local(): pl.pallas_call(functools.partial(kernel, sizes), out_shape=jax.ShapeDtype...]
where the time goes in v2:
time: 17.9 us; the launch traced here: 17.7 us
  Pallas kernels  17 us (95%)
  local copies, waits for them, and re-layouts  0.67 us (4%)
    pallas_call x1, Pallas kernels, local(): pl.pallas_call(functools.partial(kernel, sizes), out_shape=jax.ShapeDtype...  17 us
    unnamed x1, local copies, waits for them, and re-layouts  0.67 us

profile of v2, /device:TPU:0, one launch (start us, length us, event | category | flops | bytes accessed | tf_op | source)
XLA Modules:
  0.0 17.7 jit_solution(7501885655121011493)
XLA Ops:
  0.0 17.0 %shard_map.73 = f32[5,2,16,256]{3,2,1,0:T(8,128)S(1)} custom-call(f32[5,2,16,256]{3,2,1,0:T(8,128)} %state_hbm.1, f32[9,2,16,256]{3,2,1,0:T(8,128)} %metrics_hbm.1, f32[2,16,256]{2,1,0:T(8,128)} %volume_hbm.1, s32[2,16,256]{2,1,0:T(8,128)} %blank_hbm.1, s32[1,8,256]{2,1,0:T(8,128)} %cells_hbm.1, f32[3,1,256]{2,1,0:T(1,128)} %bitcast.1, s32[1,256]{1,0:T(1,128)} %targets_hbm.1), custom_call_target="tpu_custom_call" | custom-call | tf_op jit(solution)/shard_map/pallas_call | solution.py:402
  17.0 0.7 %copy.9 = f32[5,2,16,256]{3,2,1,0:T(8,128)} copy(f32[5,2,16,256]{3,2,1,0:T(8,128)S(1)} %shard_map.73) | data formatting | bytes 327680

commit v3 on v2

--- a/solution.py
+++ b/solution.py
@@ -14,12 +14,10 @@
 MESH = pl.DeviceIdType.MESH
 
 
-def split3(x):
+def split2(x):
     high = x.astype(jnp.bfloat16)
     rest = x - high.astype(jnp.float32)
-    middle = rest.astype(jnp.bfloat16)
-    low = (rest - middle.astype(jnp.float32)).astype(jnp.bfloat16)
-    return high, middle, low
+    return high, rest.astype(jnp.bfloat16)
 
 
 def primitive(u):
@@ -121,13 +119,13 @@
             )
         )
     ]
-    for load in loads:
-        load.start()
     barrier = pltpu.get_barrier_semaphore()
     for d in range(1, n):
         pl.semaphore_signal(
             barrier, inc=1, device_id=peer(lax.rem(me + d, n)), device_id_type=MESH
         )
+    for load in loads:
+        load.start()
 
     def row_of(index, length):
         return lax.broadcasted_iota(jnp.int32, (length, slots), 0) == index
@@ -155,7 +153,7 @@
     def gather(source, step):
         rows = nvar * planes * columns
         flat = source[...].reshape(rows, depth)
-        parts = split3(flat)
+        parts = split2(flat)
         picked = sum(
             jnp.dot(part, hot[...], preferred_element_type=jnp.float32) for part in parts[::-1]
         )
@@ -253,7 +251,7 @@
                 normals[g, i, x] = mean[x]
 
     def spread_of(index, cell):
-        spread[index] = one_hot(cell % depth, depth).astype(jnp.bfloat16)
+        spread[index] = one_hot(cell % depth, depth).T.astype(jnp.bfloat16)
 
     spread_of(0, targets[...])
     for load in loads[5:]:
@@ -267,11 +265,10 @@
         halo_targets[1] // depth,
     ]
     rows_of = [planes * columns, columns, columns]
-    nt = (((1,), (1,)), ((), ()))
     fringe = []
     for t in range(3):
-        found = lax.dot_general(
-            one_hot(place_rows[t], rows_of[t]).astype(jnp.bfloat16), spread[t], nt,
+        found = jnp.dot(
+            one_hot(place_rows[t], rows_of[t]).astype(jnp.bfloat16), spread[t],
             preferred_element_type=jnp.float32,
         )
         fringe.append(found > 0.5)
@@ -309,7 +306,7 @@
     def fill(step, t, values, current):
         mine = row_of(place_rows[t], rows_of[t])
         parts = []
-        for part in split3(values):
+        for part in split2(values):
             wide = part.astype(jnp.float32)
             parts.append(
                 jnp.concatenate(
@@ -317,7 +314,7 @@
                 ).astype(jnp.bfloat16)
             )
         placed = sum(
-            lax.dot_general(part, spread[t], nt, preferred_element_type=jnp.float32)
+            jnp.dot(part, spread[t], preferred_element_type=jnp.float32)
             for part in parts[::-1]
         )
         out = []
@@ -339,13 +336,13 @@
         return [[ref[v, i] for v in range(nvar)] for i in range(planes)]
 
     def section(step, source, halo_pairs):
+        both_sides(halo_pairs, "wait_recv")
         drain(step, recv_sem)
         values = arrived(step)
         own = fill(step, 0, values[0], planes_of(source))
         for i in range(planes):
             for v in range(nvar):
                 filled[step, v, i] = own[i][v]
-        both_sides(halo_pairs, "wait_recv")
         left = fill(step, 1, values[1], [[halo[step, 0, v] for v in range(nvar)]])[0]
         right = fill(step, 2, values[2], [[halo[step, 1, v] for v in range(nvar)]])[0]
         left = [jnp.where(has_left, a, b) for a, b in zip(left, own[0])]
@@ -413,7 +410,7 @@
             pltpu.VMEM((3, 1, slots), f32),
             pltpu.VMEM(receiver_cells.shape, i32),
             pltpu.VMEM((depth, 2 * slots), bf16),
-            pltpu.VMEM((3, depth, slots), bf16),
+            pltpu.VMEM((3, slots, depth), bf16),
             pltpu.VMEM((2, tiles, 8, LANES), f32),
             pltpu.VMEM((2, n, 8, LANES), f32),
             pltpu.VMEM((2, 2, nvar, columns, depth), f32),

time: 17.9 us -> 17.2 us (0.961)
  Pallas kernels: 17 us -> 16.3 us
    pallas_call x1, Pallas kernels: 17 us -> 16.3 us  [local(): pl.pallas_call(functools.partial(kernel, sizes), out_shape=jax.ShapeDtype...]
where the time goes in v3:
time: 17.2 us; the launch traced here: 17 us
  Pallas kernels  16.3 us (95%)
  local copies, waits for them, and re-layouts  0.67 us (4%)
    pallas_call x1, Pallas kernels, local(): pl.pallas_call(functools.partial(kernel, sizes), out_shape=jax.ShapeDtype...  16.3 us
    unnamed x1, local copies, waits for them, and re-layouts  0.67 us

profile of v3, /device:TPU:0, one launch (start us, length us, event | category | flops | bytes accessed | tf_op | source)
XLA Modules:
  0.0 17.0 jit_solution(11374872522705308674)
XLA Ops:
  0.0 16.3 %shard_map.73 = f32[5,2,16,256]{3,2,1,0:T(8,128)S(1)} custom-call(f32[5,2,16,256]{3,2,1,0:T(8,128)} %state_hbm.1, f32[9,2,16,256]{3,2,1,0:T(8,128)} %metrics_hbm.1, f32[2,16,256]{2,1,0:T(8,128)} %volume_hbm.1, s32[2,16,256]{2,1,0:T(8,128)} %blank_hbm.1, s32[1,8,256]{2,1,0:T(8,128)} %cells_hbm.1, f32[3,1,256]{2,1,0:T(1,128)} %bitcast.1, s32[1,256]{1,0:T(1,128)} %targets_hbm.1), custom_call_target="tpu_custom_call" | custom-call | tf_op jit(solution)/shard_map/pallas_call | solution.py:399
  16.3 0.7 %copy.9 = f32[5,2,16,256]{3,2,1,0:T(8,128)} copy(f32[5,2,16,256]{3,2,1,0:T(8,128)S(1)} %shard_map.73) | data formatting | bytes 327680

commit v4 on v3

--- a/solution.py
+++ b/solution.py
@@ -119,11 +119,18 @@
             )
         )
     ]
+    bits = n.bit_length() - 1
+    if n == 1 << bits:
+        digits = [(me // (1 << b)) % 2 for b in range(bits)]
+        others = [
+            sum(((1 - digits[b]) if (mask >> b) % 2 else digits[b]) * (1 << b) for b in range(bits))
+            for mask in range(n - 1, 0, -1)
+        ]
+    else:
+        others = [lax.rem(me + d, n) for d in range(1, n)]
     barrier = pltpu.get_barrier_semaphore()
-    for d in range(1, n):
-        pl.semaphore_signal(
-            barrier, inc=1, device_id=peer(lax.rem(me + d, n)), device_id_type=MESH
-        )
+    for r in others:
+        pl.semaphore_signal(barrier, inc=1, device_id=peer(r), device_id_type=MESH)
     for load in loads:
         load.start()
 
@@ -169,8 +176,7 @@
 
     def exchange(step):
         copies = []
-        for d in range(1, n):
-            r = lax.rem(me + d, n)
+        for r in others:
             copies.append(
                 pltpu.make_async_remote_copy(
                     src_ref=send.at[step, r // per],
@@ -374,9 +380,9 @@
         for v in range(nvar):
             middle[v, i] = filled[0, v, i] + jnp.where(update, change[v], 0.0)
     halo_1 = [[copy] for copy in halo_copies(middle, 1)]
-    both_sides(halo_1, "start")
     gather(middle, 1)
     exchange(1)
+    both_sides(halo_1, "start")
     for i, (update, change) in enumerate(section(1, middle, halo_1)):
         for v in range(nvar):
             end = filled[1, v, i]

time: 17.2 us -> 16.8 us (0.977)
  Pallas kernels: 16.3 us -> 15.9 us
    pallas_call x1, Pallas kernels: 16.3 us -> 15.9 us  [local(): pl.pallas_call(functools.partial(kernel, sizes), out_shape=jax.ShapeDtype...]
where the time goes in v4:
time: 16.8 us; the launch traced here: 16.6 us
  Pallas kernels  15.9 us (95%)
  local copies, waits for them, and re-layouts  0.67 us (4%)
    pallas_call x1, Pallas kernels, local(): pl.pallas_call(functools.partial(kernel, sizes), out_shape=jax.ShapeDtype...  15.9 us
    unnamed x1, local copies, waits for them, and re-layouts  0.67 us

profile of v4, /device:TPU:0, one launch (start us, length us, event | category | flops | bytes accessed | tf_op | source)
XLA Modules:
  0.0 16.6 jit_solution(13044948418572946682)
XLA Ops:
  0.0 15.9 %shard_map.73 = f32[5,2,16,256]{3,2,1,0:T(8,128)S(1)} custom-call(f32[5,2,16,256]{3,2,1,0:T(8,128)} %state_hbm.1, f32[9,2,16,256]{3,2,1,0:T(8,128)} %metrics_hbm.1, f32[2,16,256]{2,1,0:T(8,128)} %volume_hbm.1, s32[2,16,256]{2,1,0:T(8,128)} %blank_hbm.1, s32[1,8,256]{2,1,0:T(8,128)} %cells_hbm.1, f32[3,1,256]{2,1,0:T(1,128)} %bitcast.1, s32[1,256]{1,0:T(1,128)} %targets_hbm.1), custom_call_target="tpu_custom_call" | custom-call | tf_op jit(solution)/shard_map/pallas_call | solution.py:405
  15.9 0.7 %copy.9 = f32[5,2,16,256]{3,2,1,0:T(8,128)} copy(f32[5,2,16,256]{3,2,1,0:T(8,128)S(1)} %shard_map.73) | data formatting | bytes 327680

commit v5 on v4

--- a/solution.py
+++ b/solution.py
@@ -246,8 +246,8 @@
     exchange(0)
     once = once_copies()
     halo_0 = [[copy] for copy in halo_copies(state, 0)]
+    both_sides(once, "start")
     both_sides(halo_0, "start")
-    both_sides(once, "start")
 
     for i in range(planes):
         for g in (1, 2):

time: 16.8 us -> 16.8 us (level)
  no operation moved by 1% of the time
where the time goes in v5:
time: 16.8 us; the launch traced here: 16.6 us
  Pallas kernels  15.9 us (95%)
  local copies, waits for them, and re-layouts  0.67 us (4%)
    pallas_call x1, Pallas kernels, local(): pl.pallas_call(functools.partial(kernel, sizes), out_shape=jax.ShapeDtype...  15.9 us
    unnamed x1, local copies, waits for them, and re-layouts  0.67 us

profile of v5, /device:TPU:0, one launch (start us, length us, event | category | flops | bytes accessed | tf_op | source)
XLA Modules:
  0.0 16.6 jit_solution(17460697357882741406)
XLA Ops:
  0.0 15.9 %shard_map.73 = f32[5,2,16,256]{3,2,1,0:T(8,128)S(1)} custom-call(f32[5,2,16,256]{3,2,1,0:T(8,128)} %state_hbm.1, f32[9,2,16,256]{3,2,1,0:T(8,128)} %metrics_hbm.1, f32[2,16,256]{2,1,0:T(8,128)} %volume_hbm.1, s32[2,16,256]{2,1,0:T(8,128)} %blank_hbm.1, s32[1,8,256]{2,1,0:T(8,128)} %cells_hbm.1, f32[3,1,256]{2,1,0:T(1,128)} %bitcast.1, s32[1,256]{1,0:T(1,128)} %targets_hbm.1), custom_call_target="tpu_custom_call" | custom-call | tf_op jit(solution)/shard_map/pallas_call | solution.py:405
  15.9 0.7 %copy.9 = f32[5,2,16,256]{3,2,1,0:T(8,128)} copy(f32[5,2,16,256]{3,2,1,0:T(8,128)S(1)} %shard_map.73) | data formatting | bytes 327680
